TPU v7x, 32 devices: a whole 2x2x4 slice. The times are simulated.
32 devices in a mesh: ctx: 8 (over z, y), tp: 4 (over x, core).
Axes of the slice: x: 2, y: 2, z: 4, core: 2. Of those that a mesh axis runs over, the one named last changes fastest.
Arguments:
- residual: bfloat16 [2048, 8192], P('ctx', 'tp'), may hold values from -90 to 90
- hyena_gate: bfloat16 [2048, 8192], P('ctx', 'tp'), may hold values from -6 to 6
- hyena_key: bfloat16 [2048, 8192], P('ctx', 'tp'), may hold values from -6 to 6
- hyena_value: bfloat16 [2048, 8192], P('ctx', 'tp'), may hold values from -6 to 6
- filter_taps: float32 [512, 128], P('tp'), may hold values from -0.45 to 0.45
- norm_gain: float32 [8192], P('tp'), may hold values from 0.5 to 1.5
- att_query: bfloat16 [2048, 8192], P('ctx', 'tp'), may hold values from -180 to 180
- att_key: bfloat16 [2048, 8192], P('ctx', 'tp'), may hold values from -6 to 6
- att_value: bfloat16 [2048, 8192], P('ctx', 'tp'), may hold values from -6 to 6
- doc_lengths: int32 [8], replicated, may hold values from 1 to 768, 2048 in all
Outputs:
- normed: bfloat16 [2048, 8192], P('ctx', 'tp')
- attended: bfloat16 [2048, 8192], P('ctx', 'tp')
Inputs may be any that keep to these rules, and one draw needn't show every extreme that they name: `doc_lengths`: the lengths sum to 2048; the longest document has exactly 768 tokens.
All inputs are finite; a program needn't handle non-finite values.
Results may differ from a plain program's by a relative error of at most 0.0075.
Values may be sent and summed in bfloat16 or wider, within the bound.
A program may use at most 128 MiB of HBM per device.

v0:
```python
import jax
import jax.numpy as jnp
from jax import lax
from jax.sharding import PartitionSpec as P

D = 8192
HEAD_DIM = 128
REACH = 3


norm_epsilon = 1e-05


def shifted(value, axis, steps):
    count = lax.axis_size(axis)
    first, last = (max(0, -steps), min(count, count - steps))
    return lax.ppermute(value, axis, [(source, source + steps) for source in range(first, last)])


def document_begin(doc_lengths, positions):
    count = doc_lengths.shape[0]
    order = jnp.arange(count, dtype=jnp.int32)
    before = order[None, :] < order[:, None]
    starts = jnp.sum(jnp.where(before, doc_lengths[None, :], 0), axis=1)
    return jnp.max(jnp.where(starts[None, :] <= positions[:, None], starts[None, :], 0), axis=1)


def causal_filter(extended, filter_taps, reach_back, out_rows):
    groups, taps = filter_taps.shape
    channels = extended.shape[1]
    width = channels // groups
    lag_table = (
        jnp.arange(taps, dtype=jnp.int32)[:, None]
        + (taps - 1)
        - jnp.arange(2 * taps - 1, dtype=jnp.int32)[None, :]
    )
    reversed_taps = filter_taps[:, ::-1]
    period = jnp.concatenate([reversed_taps, jnp.zeros((groups, taps), jnp.float32)], axis=1)
    tiled = jnp.tile(period, (1, taps))
    toeplitz = tiled[:, : taps * (2 * taps - 1)].reshape(groups, taps, 2 * taps - 1)
    upper_part = toeplitz.astype(jnp.bfloat16)
    lower_part = (toeplitz - upper_part.astype(jnp.float32)).astype(jnp.bfloat16)
    zero_half = jnp.zeros((), jnp.bfloat16)
    numbers = (((0,), (2,)), ((1,), (0,)))
    results = []
    for block_index in range(out_rows // taps):
        first = block_index * taps
        sources = extended[first : first + 2 * taps - 1].reshape(2 * taps - 1, groups, width)
        limits = reach_back[first : first + taps]
        valid = (lag_table <= limits[:, None])[None]
        kernel_upper = jnp.where(valid, upper_part, zero_half)
        kernel_lower = jnp.where(valid, lower_part, zero_half)
        result = lax.dot_general(sources, kernel_upper, numbers, preferred_element_type=jnp.float32)
        result = result + lax.dot_general(
            sources, kernel_lower, numbers, preferred_element_type=jnp.float32
        )
        results.append(result.transpose(2, 0, 1).reshape(taps, channels))
    return jnp.concatenate(results, axis=0)


def attend_one(query_head, key_head, value_head, visible, scale):
    scores = (
        lax.dot_general(
            query_head, key_head, (((1,), (1,)), ((), ())), preferred_element_type=jnp.float32
        )
        * scale
    )
    scores = jnp.where(visible, scores, jnp.float32(-1e30))
    top = jnp.max(scores, axis=1, keepdims=True)
    expo = jnp.where(visible, jnp.exp(scores - top), jnp.float32(0.0))
    denominator = jnp.sum(expo, axis=1, keepdims=True)
    summed = jnp.dot(expo.astype(jnp.bfloat16), value_head, preferred_element_type=jnp.float32)
    return (summed / denominator).astype(jnp.bfloat16)


def on_device(
    residual,
    hyena_gate,
    hyena_key,
    hyena_value,
    filter_taps,
    norm_gain,
    att_query,
    att_key,
    att_value,
    doc_lengths,
):
    tok_rows = residual.shape[0]
    taps = filter_taps.shape[1]
    shard_index = lax.axis_index("ctx")
    anchor = shard_index * tok_rows
    positions = anchor + jnp.arange(tok_rows, dtype=jnp.int32)
    doc_begin = document_begin(doc_lengths, positions)
    mixed_rows = (hyena_key.astype(jnp.float32) * hyena_value.astype(jnp.float32)).astype(
        jnp.bfloat16
    )
    rim_rows = shifted(mixed_rows[tok_rows - (taps - 1) :], "ctx", 1)
    extended = jnp.concatenate([rim_rows, mixed_rows], axis=0)
    filtered = causal_filter(extended, filter_taps, positions - doc_begin, tok_rows)
    hidden = residual.astype(jnp.float32) + hyena_gate.astype(jnp.float32) * filtered
    local_sum = jnp.sum(hidden * hidden, axis=1)
    mean_square = lax.psum(local_sum, "tp") / D
    normed = (hidden * lax.rsqrt(mean_square + norm_epsilon)[:, None] * norm_gain[None, :]).astype(
        jnp.bfloat16
    )
    key_pair = jnp.stack([att_key, att_value])
    pieces = [shifted(key_pair, "ctx", distance) for distance in range(REACH, 0, -1)]
    key_rows = jnp.concatenate([piece[0] for piece in pieces] + [att_key], axis=0)
    value_rows = jnp.concatenate([piece[1] for piece in pieces] + [att_value], axis=0)
    window = key_rows.shape[0]
    key_pos = anchor - REACH * tok_rows + jnp.arange(window, dtype=jnp.int32)
    visible = (key_pos[None, :] <= positions[:, None]) & (key_pos[None, :] >= doc_begin[:, None])
    scale = jnp.float32(1.0 / HEAD_DIM**0.5)
    head_count = att_query.shape[1] // HEAD_DIM
    outputs = []
    for head_index in range(head_count):
        lower = head_index * HEAD_DIM
        upper = lower + HEAD_DIM
        outputs.append(
            attend_one(
                att_query[:, lower:upper],
                key_rows[:, lower:upper],
                value_rows[:, lower:upper],
                visible,
                scale,
            )
        )
    attended = jnp.concatenate(outputs, axis=1)
    return (normed, attended)


def solution(mesh):
    placed = (
        P("ctx", "tp"),
        P("ctx", "tp"),
        P("ctx", "tp"),
        P("ctx", "tp"),
        P("tp", None),
        P("tp"),
        P("ctx", "tp"),
        P("ctx", "tp"),
        P("ctx", "tp"),
        P(),
    )
    return jax.shard_map(
        on_device,
        mesh=mesh,
        in_specs=placed,
        out_specs=(P("ctx", "tp"), P("ctx", "tp")),
        check_vma=False,
    )
```

profile of v0, /device:TPU:18, one launch (start us, length us, event | category | flops | bytes accessed | tf_op | source)
XLA Modules:
  0.0 281.1 jit_solution(4953669906663487611)
XLA Ops:
  0.7 3.2 %pad_maximum_fusion.2 = bf16[2,256,2048]{2,1,0:T(8,128)(2,1)} fusion(bf16[1,256,2048]{2,1,0:T(8,128)(2,1)} %bitcast.101, bf16[1,256,2048]{2,1,0:T(8,128)(2,1)} %bitcast.100), kind=kLoop, calls=%fused_computation.21 | loop fusion | flops 1048576 | bytes 4194304 | tf_op jit(solution)/shard_map/stack | solution.py:106
  3.9 3.4 %collective-permute-start.3 = (bf16[2,256,2048]{2,1,0:T(8,128)(2,1)}, bf16[2,256,2048]{2,1,0:T(8,128)(2,1)}, u32[]{:S(2)}, u32[]{:S(2)}) collective-permute-start(bf16[2,256,2048]{2,1,0:T(8,128)(2,1)} %pad_maximum_fusion.2), channel_id=1, source_target_pairs={{0,4},{4,8},{8,12},{12,16},{16,20},{20,24},{24,28},{1,5},{5,9},{9,... | collective-permute-start | bytes 6291464 | tf_op jit(solution)/shard_map/ppermute | solution.py:17
  7.3 3.5 %collective-permute-start.2 = (bf16[2,256,2048]{2,1,0:T(8,128)(2,1)}, bf16[2,256,2048]{2,1,0:T(8,128)(2,1)}, u32[]{:S(2)}, u32[]{:S(2)}) collective-permute-start(bf16[2,256,2048]{2,1,0:T(8,128)(2,1)} %pad_maximum_fusion.2), channel_id=1, source_target_pairs={{0,8},{4,12},{8,16},{12,20},{16,24},{20,28},{1,9},{5,13},{9,17},{1... | collective-permute-start | bytes 6291464 | tf_op jit(solution)/shard_map/ppermute | solution.py:17
  10.8 1.9 collective-permute-start.1
  12.7 0.4 multiply_convert_fusion.1
  13.3 1.9 collective-permute-start
  15.6 1.3 tile.4
  16.9 20.7 %copy.27 = f32[16,8,128,256]{3,1,2,0:T(8,128)S(1)} copy(f32[16,8,128,256]{3,2,1,0:T(8,128)S(1)} %bitcast.92) | data formatting | bytes 33554432
  37.6 6.0 %slice.241 = f32[128,32640]{1,0:T(8,128)} slice(f32[128,32768]{1,0:T(8,128)S(1)} %bitcast.93), slice={[0:128], [0:32640]} | slice | bytes 33423360 | tf_op jit(solution)/shard_map/slice | solution.py:40
  43.5 28.9 %reshape.134 = f32[128,128,255]{2,1,0:T(8,128)} reshape(f32[128,32640]{1,0:T(8,128)} %slice.241) | data formatting | bytes 33423360 | tf_op jit(solution)/shard_map/reshape | solution.py:40
  72.5 0.7 fusion.200
  73.2 127.2 %collective-permute-done = bf16[127,2048]{1,0:T(8,128)(2,1)} collective-permute-done((bf16[127,2048]{1,0:T(8,128)(2,1)S(1)}, bf16[127,2048]{1,0:T(8,128)(2,1)}, u32[]{:S(2)}, u32[]{:S(2)}) %collective-permute-start) | collective-permute-done | bytes 520224 | tf_op jit(solution)/shard_map/ppermute | solution.py:17
  200.4 1.4 pad_maximum_fusion.3
  201.8 1.3 copy.23
  203.1 0.7 copy.22
  203.8 14.3 %fusion = f32[128,16,128]{2,1,0:T(8,128)} fusion(bf16[255,128,16]{0,2,1:T(8,128)(2,1)} %bitcast.96, pred[128,255]{1,0:T(8,128)(4,1)} %get-tuple-element.35, f32[128,128,255]{2,1,0:T(8,128)} %reshape.134), kind=kOutput, calls=%fused_computation.1 | convolution fusion | flops 154583040 | bytes 18837376 | tf_op jit(solution)/shard_map/dot_general | solution.py:54
  218.1 1.7 copy-done
  219.8 4.0 %fusion.4 = f32[128,16,128]{2,1,0:T(8,128)} fusion(bf16[255,128,16]{0,2,1:T(8,128)(2,1)S(1)} %bitcast.94, pred[128,255]{1,0:T(8,128)(4,1)} %get-tuple-element.34, f32[128,128,255]{2,1,0:T(8,128)S(1)} %copy-done), kind=kOutput, calls=%fused_computation.5 | convolution fusion | flops 154583040 | bytes 18837376 | tf_op jit(solution)/shard_map/dot_general | solution.py:54
  223.9 8.7 %fusion.52 = f32[128,16,128]{2,1,0:T(8,128)S(1)} fusion(f32[128,16,128]{2,1,0:T(8,128)} %fusion, bf16[255,128,16]{0,2,1:T(8,128)(2,1)} %bitcast.97, pred[128,255]{1,0:T(8,128)(4,1)} %get-tuple-element.35, f32[128,128,255]{2,1,0:T(8,128)} %reshape.134), kind=kOutput, calls=%fused_computation.74 | convolution fusion | flops 142311424 | bytes 19885952 | tf_op jit(solution)/shard_map/dot_general | solution.py:53
  232.6 9.0 %fusion.49 = f32[128,16,128]{2,1,0:T(8,128)} fusion(f32[128,16,128]{2,1,0:T(8,128)S(1)} %copy-done.1, bf16[255,128,16]{0,2,1:T(8,128)(2,1)S(1)} %bitcast.95, pred[128,255]{1,0:T(8,128)(4,1)S(1)} %copy-done.7, f32[128,128,255]{2,1,0:T(8,128)} %reshape.134), kind=kOutput, calls=%fused_computation.73 | convolution fusion | flops 142311424 | bytes 19885952 | tf_op jit(solution)/shard_map/dot_general | solution.py:53
  241.6 0.3 copy.25
  241.9 1.6 copy.24
  243.5 1.7 multiply_reduce_fusion
  245.2 5.9 %psum.7 = f32[256]{0:T(256)S(1)} all-reduce(f32[256]{0:T(256)S(1)} %multiply_reduce_fusion), channel_id=1, replica_groups=mesh['ctx'=8,'tp'=4] {'tp'}, use_global_device_ids=true, to_apply=%region_3.4 | all-reduce | flops 256 | bytes 2048 | tf_op jit(solution)/shard_map/psum | solution.py:102
  251.2 2.7 multiply_convert_fusion
  253.9 1.7 slice_bitcast_fusion
  255.6 1.8 slice_bitcast_fusion.1
  257.4 1.7 slice_bitcast_fusion.2
  259.1 1.9 pad_maximum_fusion
  261.0 0.4 fusion.241
  261.4 0.4 fusion.242
  261.8 0.4 fusion.243
  262.2 0.4 fusion.244
  262.7 0.4 fusion.245
  263.1 0.4 fusion.246
  263.5 0.4 fusion.247
  263.9 0.4 fusion.248
  264.3 0.4 fusion.249
  264.7 0.4 fusion.250
  265.1 0.4 fusion.251
  265.5 0.4 fusion.252
  265.9 0.4 fusion.253
  266.3 0.4 fusion.254
  266.7 0.4 fusion.255
  267.1 0.4 fusion.256
  267.5 1.9 fusion.117
  269.4 0.5 fusion.56
  269.9 0.5 fusion.58
  270.4 0.5 fusion.60
  270.9 0.5 fusion.62
  271.4 0.5 fusion.64
  271.9 0.5 fusion.66
  272.4 0.5 fusion.68
  272.9 2.2 fusion.115
  275.1 0.5 fusion.70
  275.6 0.5 fusion.72
  276.1 0.5 fusion.74
  276.6 0.5 fusion.76
  277.1 0.5 fusion.78
  277.6 0.5 fusion.80
  278.1 0.5 fusion.82
  278.6 0.5 fusion.84
  279.1 0.5 fusion.86
  279.6 1.4 copy.26
  (36 shorter events, 0.5 us)
Async XLA Ops:
  0.6 12.1 %copy-start.5 = (bf16[256,2048]{1,0:T(8,128)(2,1)S(1)}, bf16[256,2048]{1,0:T(8,128)(2,1)}, u32[]{:S(2)}) copy-start(bf16[256,2048]{1,0:T(8,128)(2,1)} %param.13) | copy-start | bytes 3145732
  0.6 12.1 %copy-start.6 = (bf16[256,2048]{1,0:T(8,128)(2,1)S(1)}, bf16[256,2048]{1,0:T(8,128)(2,1)}, u32[]{:S(2)}) copy-start(bf16[256,2048]{1,0:T(8,128)(2,1)} %param.12) | copy-start | bytes 3145732
  0.7 14.6 %copy-start.11 = (s32[8]{0:T(128)S(1)}, s32[8]{0:T(128)}, u32[]{:S(2)}) copy-start(s32[8]{0:T(128)} %param.19) | copy-start | bytes 100
  0.7 14.8 %copy-start.8 = (f32[128,128]{1,0:T(8,128)S(1)}, f32[128,128]{1,0:T(8,128)}, u32[]{:S(2)}) copy-start(f32[128,128]{1,0:T(8,128)} %param.14) | copy-start | bytes 196612
  3.9 250.0 %collective-permute-start.3 = (bf16[2,256,2048]{2,1,0:T(8,128)(2,1)}, bf16[2,256,2048]{2,1,0:T(8,128)(2,1)}, u32[]{:S(2)}, u32[]{:S(2)}) collective-permute-start(bf16[2,256,2048]{2,1,0:T(8,128)(2,1)} %pad_maximum_fusion.2), channel_id=1, source_target_pairs={{0,4},{4,8},{8,12},{12,16},{16,20},{20,24},{24,28},{1,5},{5,9},{9,... | collective-permute-start | bytes 6291464 | tf_op jit(solution)/shard_map/ppermute | solution.py:17
  7.3 248.3 %collective-permute-start.2 = (bf16[2,256,2048]{2,1,0:T(8,128)(2,1)}, bf16[2,256,2048]{2,1,0:T(8,128)(2,1)}, u32[]{:S(2)}, u32[]{:S(2)}) collective-permute-start(bf16[2,256,2048]{2,1,0:T(8,128)(2,1)} %pad_maximum_fusion.2), channel_id=1, source_target_pairs={{0,8},{4,12},{8,16},{12,20},{16,24},{20,28},{1,9},{5,13},{9,17},{1... | collective-permute-start | bytes 6291464 | tf_op jit(solution)/shard_map/ppermute | solution.py:17
  10.8 246.6 %collective-permute-start.1 = (bf16[2,256,2048]{2,1,0:T(8,128)(2,1)}, bf16[2,256,2048]{2,1,0:T(8,128)(2,1)}, u32[]{:S(2)}, u32[]{:S(2)}) collective-permute-start(bf16[2,256,2048]{2,1,0:T(8,128)(2,1)} %pad_maximum_fusion.2), channel_id=1, source_target_pairs={{0,12},{4,16},{8,20},{12,24},{16,28},{1,13},{5,17},{9,21},{13,25},... | collective-permute-start | bytes 6291464 | tf_op jit(solution)/shard_map/ppermute | solution.py:17
  13.3 187.1 %collective-permute-start = (bf16[127,2048]{1,0:T(8,128)(2,1)S(1)}, bf16[127,2048]{1,0:T(8,128)(2,1)}, u32[]{:S(2)}, u32[]{:S(2)}) collective-permute-start(bf16[127,2048]{1,0:T(8,128)(2,1)S(1)} %slice.240), channel_id=1, source_target_pairs={{0,4},{4,8},{8,12},{12,16},{16,20},{20,24},{24,28},{1,5},{5,9},{9,... | collective-permute-start | bytes 1560584 | tf_op jit(solution)/shard_map/ppermute | solution.py:17
  203.8 16.0 %copy-start = (f32[128,128,255]{2,1,0:T(8,128)S(1)}, f32[128,128,255]{2,1,0:T(8,128)}, u32[]{:S(2)}) copy-start(f32[128,128,255]{2,1,0:T(8,128)} %reshape.134) | copy-start | bytes 50135044
  223.9 8.7 %copy-start.1 = (f32[128,16,128]{2,1,0:T(8,128)S(1)}, f32[128,16,128]{2,1,0:T(8,128)}, u32[]{:S(2)}) copy-start(f32[128,16,128]{2,1,0:T(8,128)} %fusion.4) | copy-start | bytes 3145732
  223.9 8.7 %copy-start.7 = (pred[128,255]{1,0:T(8,128)(4,1)S(1)}, pred[128,255]{1,0:T(8,128)(4,1)}, u32[]{:S(2)}) copy-start(pred[128,255]{1,0:T(8,128)(4,1)} %get-tuple-element.34) | copy-start | bytes 97924
  241.6 1.9 copy-start.2
  241.6 9.5 %copy-start.9 = (f32[2048]{0:T(1024)S(1)}, f32[2048]{0:T(1024)}, u32[]{:S(2)}) copy-start(f32[2048]{0:T(1024)} %param.15) | copy-start | bytes 24580
  255.6 3.6 %copy-start.3 = (bf16[256,2048]{1,0:T(8,128)(2,1)S(1)}, bf16[256,2048]{1,0:T(8,128)(2,1)}, u32[]{:S(2)}) copy-start(bf16[256,2048]{1,0:T(8,128)(2,1)} %param.17) | copy-start | bytes 3145732
  255.6 3.6 %copy-start.4 = (bf16[256,2048]{1,0:T(8,128)(2,1)S(1)}, bf16[256,2048]{1,0:T(8,128)(2,1)}, u32[]{:S(2)}) copy-start(bf16[256,2048]{1,0:T(8,128)(2,1)} %param.18) | copy-start | bytes 3145732
  259.1 1.9 copy-start.10
where the time goes:
time: 282 us; the launch traced here: 281 us
  waiting for transfers between devices  127 us (45%)
  local copies, waits for them, and re-layouts  69.4 us (25%)
  matrix products  50.3 us (18%)
  other arithmetic  16.4 us (6%)
  starting transfers between devices  10.7 us (4%)
  blocking collectives  5.9 us (2%)
    ppermute x4, waiting for transfers between devices, shifted(): lax.ppermute(value, axis, [(source, source + steps) for source in range(f...  127 us
    reshape x1, local copies, waits for them, and re-layouts, causal_filter(): tiled[:, :taps * (2 * taps - 1)].reshape(groups, taps, 2 * taps - 1)  28.9 us
    unnamed x26, local copies, waits for them, and re-layouts  23.9 us
    dot_general x2, matrix products, causal_filter(): lax.dot_general(sources, kernel_lower, numbers, preferred_element_type=jn...  18.3 us
    dot_general x2, matrix products, causal_filter(): lax.dot_general(sources, kernel_upper, numbers, preferred_element_type=jn...  17.7 us
    ppermute x4, starting transfers between devices, shifted(): lax.ppermute(value, axis, [(source, source + steps) for source in range(f...  10.7 us
    dot_general x16, matrix products, attend_one(): jnp.dot(expo.astype(jnp.bfloat16), value_head, preferred_element_type=jnp...  7.9 us
    dot_general x16, matrix products, attend_one(): lax.dot_general(query_head, key_head, (((1,), (1,)), ((), ())), preferred...  6.38 us
  transfers between devices with their start and end apart: 4, of which 1 were waited for; matrix products, arithmetic and copies ran while one was open for 38% of the time, Pallas kernels for 0%

commit v1 on v0

v1 whole, which is shorter than its diff:
```python
import functools

import jax
import jax.numpy as jnp
from jax import lax
from jax.experimental import pallas as pl
from jax.experimental.pallas import tpu as pltpu
from jax.sharding import PartitionSpec as P

HEAD_DIM = 128
REACH = 3
LANES = 128
EPSILON = 1e-05
MESH = pl.DeviceIdType.MESH


def kernel(
    model_width,
    res_ref,
    gate_ref,
    hkey_ref,
    hval_ref,
    base_ref,
    gain_ref,
    query_ref,
    key_ref,
    value_ref,
    docs_ref,
    normed_ref,
    attended_ref,
    pairs,
    extended,
    hidden,
    squares,
    bias,
    keep,
    send_sem,
    recv_sem,
    rim_send,
    rim_recv,
    sum_send,
    sum_recv,
):
    shards = lax.axis_size("ctx")
    splits = lax.axis_size("tp")
    me = lax.axis_index("ctx")
    part = lax.axis_index("tp")
    rows, width = res_ref.shape
    taps = keep.shape[1]
    window = (REACH + 1) * rows
    tiles = width // LANES
    chunk = 2 * HEAD_DIM
    chunks = width // chunk
    even = lax.rem(me, 2) == 0
    odd = lax.rem(me, 2) == 1

    barrier = pltpu.get_barrier_semaphore()
    for step in (-2, -1, 1, 2):
        @pl.when((me + step >= 0) & (me + step < shards))
        def _():
            pl.semaphore_signal(barrier, inc=1, device_id={"ctx": me + step}, device_id_type=MESH)
    for step in range(1, splits):
        pl.semaphore_signal(
            barrier, inc=1, device_id={"tp": lax.rem(part + step, splits)}, device_id_type=MESH
        )

    pairs[0, REACH] = key_ref[...]
    pairs[1, REACH] = value_ref[...]
    extended[taps:, :] = (
        hkey_ref[...].astype(jnp.float32) * hval_ref[...].astype(jnp.float32)
    ).astype(jnp.bfloat16)

    @pl.when(me == 0)
    def _():
        extended[:taps, :] = jnp.zeros((taps, width), jnp.bfloat16)

    for distance in range(1, REACH + 1):
        @pl.when(me < distance)
        def _():
            pairs[0, REACH - distance] = jnp.zeros((rows, width), jnp.bfloat16)
            pairs[1, REACH - distance] = jnp.zeros((rows, width), jnp.bfloat16)

    pl.semaphore_wait(
        barrier, jnp.minimum(me, 2) + jnp.minimum(shards - 1 - me, 2) + splits - 1
    )

    def hop(kind, index, source, target, where):
        columns = pl.ds(pl.multiple_of(index * chunk, chunk), chunk)
        return pltpu.make_async_remote_copy(
            src_ref=pairs.at[:, REACH - source, :, columns],
            dst_ref=pairs.at[:, REACH - target, :, columns],
            send_sem=send_sem.at[kind, index],
            recv_sem=recv_sem.at[target - 1, index],
            device_id={"ctx": where},
            device_id_type=MESH,
        )

    def arrive(distance, index):
        columns = pl.ds(pl.multiple_of(index * chunk, chunk), chunk)
        slot = pairs.at[:, REACH - distance, :, columns]
        pltpu.make_async_copy(slot, slot, recv_sem.at[distance - 1, index]).wait()

    has_next = me + 1 < shards
    has_second = me + 2 < shards
    is_first = lambda c: lax.rem(c, 2) == 0
    is_last = lambda c: lax.rem(c, 2) == 1
    always = lambda c: c >= 0
    even_hops = [
        (even & has_second, is_first, 0, 2, 2),
        (even & has_next, always, 0, 1, 1),
        (even & has_next & (me >= 2), is_first, 2, 3, 1),
        (even & has_second & (me >= 1), always, 1, 3, 2),
    ]
    odd_hops = [
        (odd & has_second, always, 0, 2, 2),
        (odd & (me >= 2), always, 2, 1, -1),
        (odd & has_second, is_last, 1, 3, 2),
        (odd & (me >= 3), is_last, 3, 2, -1),
    ]

    def start(table, kind, index):
        condition, takes, source, target, step = table[kind]

        @pl.when(condition & takes(index))
        def _():
            hop(kind, index, source, target, me + step).start()

    def relay(table, kind, index):
        condition, takes, source, target, step = table[kind]

        @pl.when(condition & takes(index))
        def _():
            hop(kind, index, source, target, me + step).start()

    rim = pltpu.make_async_remote_copy(
        src_ref=extended.at[rows : rows + taps],
        dst_ref=extended.at[0:taps],
        send_sem=rim_send,
        recv_sem=rim_recv,
        device_id={"ctx": me + 1},
        device_id_type=MESH,
    )

    @pl.when(has_next)
    def _():
        rim.start()

    def begin(index, carry):
        start(even_hops, 0, index)
        start(even_hops, 1, index)
        start(odd_hops, 0, index)
        return carry

    lax.fori_loop(0, chunks, begin, 0)

    anchor = me * rows
    place = anchor + lax.broadcasted_iota(jnp.int32, (rows, 1), 0)
    first = jnp.zeros((rows, 1), jnp.int32)
    offset = jnp.int32(0)
    for document in range(docs_ref.shape[0]):
        first = jnp.where(place >= offset, jnp.maximum(first, offset), first)
        offset = offset + docs_ref[document]
    sites = anchor - REACH * rows + lax.broadcasted_iota(jnp.int32, (rows, window), 1)
    bias[...] = jnp.where(
        (sites <= place) & (sites >= first), jnp.float32(0.0), jnp.float32(-1e30)
    )
    for block in range(rows // taps):
        span = slice(block * taps, (block + 1) * taps)
        origin = anchor + (block - 1) * taps
        sources = origin + lax.broadcasted_iota(jnp.int32, (taps, 2 * taps), 1)
        keep[block] = jnp.where(sources >= first[span], 1.0, 0.0).astype(jnp.bfloat16)

    @pl.when(me >= 1)
    def _():
        whole = extended.at[0:taps]
        pltpu.make_async_copy(whole, whole, rim_recv).wait()

    group_width = width // base_ref.shape[0]
    per_tile = LANES // group_width
    owner = lax.broadcasted_iota(jnp.int32, (taps, LANES), 1) // group_width
    squares[0] = jnp.zeros((rows, LANES), jnp.float32)

    def filter_tile(tile):
        columns = pl.ds(pl.multiple_of(tile * LANES, LANES), LANES)
        source = extended[:, columns]
        groups = base_ref[pl.ds(pl.multiple_of(tile * per_tile, per_tile), per_tile), :]
        totals = [jnp.zeros((taps, LANES), jnp.float32) for _ in range(rows // taps)]
        for group in range(per_tile):
            spread = jnp.broadcast_to(groups[group : group + 1, :], (taps, 2 * taps))
            toeplitz = pltpu.roll(spread, 0, 1, stride=1, stride_axis=0)
            upper = toeplitz.astype(jnp.bfloat16)
            lower = (toeplitz - upper.astype(jnp.float32)).astype(jnp.bfloat16)
            for block in range(rows // taps):
                mask = keep[block]
                rhs = source[block * taps : (block + 2) * taps]
                result = jnp.dot(upper * mask, rhs, preferred_element_type=jnp.float32)
                result += jnp.dot(lower * mask, rhs, preferred_element_type=jnp.float32)
                totals[block] = jnp.where(owner == group, result, totals[block])
        for block in range(rows // taps):
            span = slice(block * taps, (block + 1) * taps)
            value = (
                res_ref[span, columns].astype(jnp.float32)
                + gate_ref[span, columns].astype(jnp.float32) * totals[block]
            )
            hidden[span, columns] = value
            squares[0, span, :] += value * value

    def first_phase(index, carry):
        def some(step, inner):
            filter_tile(index * (tiles // chunks) + step)
            return inner

        lax.fori_loop(0, tiles // chunks, some, 0)

        @pl.when((me >= 2) & (odd | (even & is_first(index))))
        def _():
            arrive(2, index)

        relay(odd_hops, 1, index)
        relay(even_hops, 2, index)

        @pl.when(me >= 1)
        def _():
            arrive(1, index)

        relay(odd_hops, 2, index)
        relay(even_hops, 3, index)
        return carry

    lax.fori_loop(0, chunks, first_phase, 0)

    def exchange(step):
        return pltpu.make_async_remote_copy(
            src_ref=squares.at[0],
            dst_ref=squares.at[step],
            send_sem=sum_send.at[step],
            recv_sem=sum_recv.at[step],
            device_id={"tp": lax.rem(part + step, splits)},
            device_id_type=MESH,
        )

    for step in range(1, splits):
        exchange(step).start()
    for step in range(1, splits):
        exchange(step).wait_recv()
    total = squares[0]
    for step in range(1, splits):
        total = total + squares[step]
    mean_square = jnp.sum(total, axis=1, keepdims=True) / model_width
    inverse = lax.rsqrt(mean_square + EPSILON)

    def norm_tile(tile, carry):
        columns = pl.ds(pl.multiple_of(tile * LANES, LANES), LANES)
        normed_ref[:, columns] = (hidden[:, columns] * inverse * gain_ref[:, columns]).astype(
            jnp.bfloat16
        )
        return carry

    lax.fori_loop(0, tiles, norm_tile, 0)

    scale = jnp.float32(1.0 / HEAD_DIM**0.5)

    def attend(head):
        columns = pl.ds(pl.multiple_of(head * HEAD_DIM, HEAD_DIM), HEAD_DIM)
        keys = pairs[0, :, :, columns].reshape(window, HEAD_DIM)
        values = pairs[1, :, :, columns].reshape(window, HEAD_DIM)
        scores = lax.dot_general(
            query_ref[:, columns], keys, (((1,), (1,)), ((), ())),
            preferred_element_type=jnp.float32,
        )
        scores = scores * scale + bias[...]
        top = jnp.max(scores, axis=1, keepdims=True)
        expo = jnp.exp(scores - top)
        denominator = jnp.sum(expo, axis=1, keepdims=True)
        summed = jnp.dot(expo.astype(jnp.bfloat16), values, preferred_element_type=jnp.float32)
        attended_ref[:, columns] = (summed / denominator).astype(jnp.bfloat16)

    def second_phase(index, carry):
        @pl.when(me >= 3)
        def _():
            arrive(3, index)

        relay(odd_hops, 3, index)

        @pl.when(even & (me >= 2) & is_last(index))
        def _():
            arrive(2, index)

        for head in range(chunk // HEAD_DIM):
            attend(index * (chunk // HEAD_DIM) + head)
        return carry

    lax.fori_loop(0, chunks, second_phase, 0)

    def finish(index, carry):
        for table in (even_hops, odd_hops):
            for kind in range(4):
                condition, takes, source, target, step = table[kind]

                @pl.when(condition & takes(index))
                def _():
                    hop(kind, index, source, target, me + step).wait_send()
        return carry

    lax.fori_loop(0, chunks, finish, 0)

    @pl.when(has_next)
    def _():
        rim.wait_send()

    for step in range(1, splits):
        exchange(step).wait_send()


def on_device(
    residual, hyena_gate, hyena_key, hyena_value, filter_taps, norm_gain,
    att_query, att_key, att_value, doc_lengths,
):
    rows, width = residual.shape
    groups, taps = filter_taps.shape
    splits = lax.axis_size("tp")
    chunks = width // (2 * HEAD_DIM)
    base = jnp.concatenate(
        [
            jnp.zeros((groups, 1), jnp.float32),
            filter_taps[:, ::-1],
            jnp.zeros((groups, taps - 1), jnp.float32),
        ],
        axis=1,
    )
    in_vmem = pl.BlockSpec(memory_space=pltpu.VMEM)
    return pl.pallas_call(
        functools.partial(kernel, width * splits),
        out_shape=(
            jax.ShapeDtypeStruct((rows, width), jnp.bfloat16),
            jax.ShapeDtypeStruct((rows, width), jnp.bfloat16),
        ),
        in_specs=[in_vmem] * 9 + [pl.BlockSpec(memory_space=pltpu.SMEM)],
        out_specs=(in_vmem, in_vmem),
        scratch_shapes=[
            pltpu.VMEM((2, REACH + 1, rows, width), jnp.bfloat16),
            pltpu.VMEM((rows + taps, width), jnp.bfloat16),
            pltpu.VMEM((rows, width), jnp.float32),
            pltpu.VMEM((splits, rows, LANES), jnp.float32),
            pltpu.VMEM((rows, (REACH + 1) * rows), jnp.float32),
            pltpu.VMEM((rows // taps, taps, 2 * taps), jnp.bfloat16),
            pltpu.SemaphoreType.DMA((4, chunks)),
            pltpu.SemaphoreType.DMA((REACH, chunks)),
            pltpu.SemaphoreType.DMA,
            pltpu.SemaphoreType.DMA,
            pltpu.SemaphoreType.DMA((splits,)),
            pltpu.SemaphoreType.DMA((splits,)),
        ],
        compiler_params=pltpu.CompilerParams(
            collective_id=0, has_side_effects=True, vmem_limit_bytes=50 * 1024 * 1024
        ),
    )(
        residual, hyena_gate, hyena_key, hyena_value, base, norm_gain[None, :],
        att_query, att_key, att_value, doc_lengths,
    )


def solution(mesh):
    both = P("ctx", "tp")
    return jax.shard_map(
        on_device,
        mesh=mesh,
        in_specs=(both, both, both, both, P("tp", None), P("tp"), both, both, both, P()),
        out_specs=(both, both),
        check_vma=False,
    )
```

time: 282 us -> 103 us (0.37)
  waiting for transfers between devices: 127 us -> 0 us
  Pallas kernels: 0 us -> 97.1 us
  local copies, waits for them, and re-layouts: 69.4 us -> 4.75 us
  matrix products: 50.3 us -> 0 us
  other arithmetic: 16.4 us -> 0.1 us
  starting transfers between devices: 10.7 us -> 0 us
  blocking collectives: 5.9 us -> 0 us
    ppermute x4 -> x0, waiting for transfers between devices: 127 us -> none  [shifted(): lax.ppermute(value, axis, [(source, source + steps) for source in range(f...]
    pallas_call x0 -> x1, Pallas kernels: none -> 97.1 us  [on_device(): pl.pallas_call(functools.partial(kernel, width * splits), out_shape=(jax....]
    dot_general x36 -> x0, matrix products: 50.3 us -> none  [the longest x2 18.3 us: causal_filter(): lax.dot_general(sources, kernel_lower, numbers, preferred_element_type=jn...]
    reshape x3 -> x0, local copies, waits for them, and re-layouts: 30.8 us -> none  [the longest x1 28.9 us: causal_filter(): tiled[:, :taps * (2 * taps - 1)].reshape(groups, taps, 2 * taps - 1)]
    unnamed x26 -> x8, local copies, waits for them, and re-layouts: 23.9 us -> 3.75 us
    ppermute x4 -> x0, starting transfers between devices: 10.7 us -> none  [shifted(): lax.ppermute(value, axis, [(source, source + steps) for source in range(f...]
    slice x4 -> x0, local copies, waits for them, and re-layouts: 8.12 us -> none  [the longest x1 5.99 us: causal_filter(): tiled[:, :taps * (2 * taps - 1)].reshape(groups, taps, 2 * taps - 1)]
    reduce_sum x4 -> x0, other arithmetic: 5.98 us -> none  [the longest x2 4.15 us: attend_one(): denominator = jnp.sum(expo, axis=1, keepdims=True)]
  transfers between devices with their start and end apart: 4 -> 0, of which waited for: 1 -> 0; matrix products, arithmetic and copies ran while one was open for 38% -> 0% of each run, Pallas kernels for 0% -> 0%
where the time goes in v1:
time: 103 us
  Pallas kernels  97.1 us (94%)
  local copies, waits for them, and re-layouts  4.75 us (5%)
    pallas_call x1, Pallas kernels, on_device(): pl.pallas_call(functools.partial(kernel, width * splits), out_shape=(jax....  97.1 us
    unnamed x8, local copies, waits for them, and re-layouts  3.75 us

profile of v1, /device:TPU:18, one launch (start us, length us, event | category | flops | bytes accessed | tf_op | source)
XLA Modules:
  0.0 102.6 jit_solution(14053190612925815877)
XLA Ops:
  0.6 0.1 pad.2.clone
  0.7 0.9 rev.3
  1.6 0.0 copy-start.1
  1.6 0.0 copy-start.2
  1.7 0.1 maximum_maximum_fusion.base_ref
  1.8 0.6 copy-done.1
  2.3 0.0 copy-done.2
  2.3 0.0 copy-start
  2.3 1.2 %copy-done = bf16[256,2048]{1,0:T(8,128)(2,1)S(1)} copy-done((bf16[256,2048]{1,0:T(8,128)(2,1)S(1)}, bf16[256,2048]{1,0:T(8,128)(2,1)}, u32[]{:S(2)}) %copy-start) | copy-done | bytes 1048600
  3.6 97.1 %shard_map.113 = (bf16[256,2048]{1,0:T(8,128)(2,1)S(1)}, bf16[256,2048]{1,0:T(8,128)(2,1)S(1)}) custom-call(bf16[256,2048]{1,0:T(8,128)(2,1)S(1)} %copy-done, bf16[256,2048]{1,0:T(8,128)(2,1)} %gate_ref.1, bf16[256,2048]{1,0:T(8,128)(2,1)} %hkey_ref.1, bf16[256,2048]{1,0:T(8,128)(2,1)} %hval_ref.1, f32[128,256]{1,0:T(8,128)S(1)} %maximum_maximum_fusion.base_ref, ...), custom_call_target="tpu_custom_call" | custom-call | tf_op jit(solution)/shard_map/pallas_call | solution.py:332
  100.7 1.0 copy.14
  101.6 1.0 copy.15
  (2 shorter events, 0.0 us)
Async XLA Ops:
  1.6 0.7 copy-start.1
  1.6 0.7 copy-start.2
  2.3 1.2 %copy-start = (bf16[256,2048]{1,0:T(8,128)(2,1)S(1)}, bf16[256,2048]{1,0:T(8,128)(2,1)}, u32[]{:S(2)}) copy-start(bf16[256,2048]{1,0:T(8,128)(2,1)} %res_ref.1) | copy-start | bytes 3145732
